TPU v7x, 128 devices: a whole 4x4x4 slice. The times are simulated.
128 devices in a mesh: row: 16 (over y, x), col: 2 (over core), rhs: 4 (over z).
Axes of the slice: x: 4, y: 4, z: 4, core: 2. Of those that a mesh axis runs over, the one named last changes fastest.
Arguments:
- load_cases: bfloat16 [6, 2, 16, 256, 1024], P(None, 'col', 'row', None, 'rhs'), parts along dimension 4, may hold values from -6 to 6
- diag_inverse: bfloat16 [6, 2, 16, 256, 256], P(None, 'col', 'row')
- factor_tiles: bfloat16 [5, 2, 16, 32, 256, 256], P(None, 'col', None, 'row'), may hold values from -0.0625 to 0.0625
- targets: int32 [5, 2, 16, 32], P(None, 'col', None, 'row'), may hold values from 0 to 9, as said below
- tile_live: int32 [5, 2, 16, 32], P(None, 'col', None, 'row'), may hold values from 0 to 1, as said below
Outputs:
- solution: bfloat16 [6, 2, 16, 256, 1024], P(None, 'col', 'row', None, 'rhs'), parts along dimension 4
There are 4 independent parts, one for each index of `rhs`. A program takes and returns all parts, laid end to end along the dimension named above; an argument that names none is the same for every part. Nothing has to cross between parts.
Inputs may be any that keep to these rules, and one draw needn't show every extreme that they name: targets[l, c, q, k] is below (5 - l) * 2, so that every block row lies in a higher level. `tile_live`: in each source level every slot of the supernodes of one index c is 1.
All inputs are finite; a program needn't handle non-finite values.
Results may differ from a plain program's by a relative error of at most 0.022.
Values may be sent and summed in bfloat16 or wider, within the bound.
No kernel may reach another device: no remote copies, remote signals or barrier semaphores. Data moves between devices by JAX's collectives and lax.ppermute only.
A program may use at most 192 MiB of HBM per device.

v0:
```python
from functools import partial

import jax
import jax.numpy as jnp
from jax import lax
from jax.sharding import PartitionSpec as P


def add_updates(tiles_level, places_level, live_level, partials, shard_piece, first_row):
    products = jnp.einsum(
        "qkab,qbn->qkan", tiles_level, shard_piece, preferred_element_type=jnp.float32
    )
    return partials.at[places_level.reshape(-1)].add(products.reshape((-1,) + products.shape[2:]))


def back_terms(tiles_level, places_level, live_level, x_rows, first_row, row_count):
    gathered = x_rows[places_level]
    return jnp.einsum("qkab,qkan->qbn", tiles_level, gathered, preferred_element_type=jnp.float32)


def solve_panel(load_cases, diag_inverse, masked, places, tile_live):
    levels = load_cases.shape[0]
    columns = lax.axis_size("col")
    block_width = load_cases.shape[3]
    num_cases = load_cases.shape[4]
    partials = jnp.zeros((levels * columns, block_width, num_cases), jnp.float32)
    solved = []
    for height in range(levels):
        pending = load_cases[height, 0, 0].astype(jnp.float32)
        if height > 0:
            pending_rows = lax.slice_in_dim(
                partials, height * columns, (height + 1) * columns, axis=0
            )
            pending = (
                pending - lax.psum_scatter(pending_rows, "col", scatter_dimension=0, tiled=True)[0]
            )
        residual = pending.astype(jnp.bfloat16)
        solved_blk = jnp.dot(
            diag_inverse[height, 0, 0], residual, preferred_element_type=jnp.float32
        ).astype(jnp.bfloat16)
        solved.append(solved_blk)
        if height < levels - 1:
            folder = partial(add_updates, masked[height], places[height], tile_live[height, 0])
            partials = folder(
                partials, lax.all_gather(solved_blk[None], "row", axis=0, tiled=True), jnp.int32(0)
            )
    x_rows = jnp.zeros((levels * columns, block_width, num_cases), jnp.bfloat16)
    results = [None] * levels
    for height in reversed(range(levels)):
        pending = solved[height].astype(jnp.float32)
        if height < levels - 1:
            term_fn = partial(
                back_terms, masked[height], places[height], tile_live[height, 0], x_rows
            )
            pending = (
                pending
                - lax.psum_scatter(
                    term_fn(jnp.int32(0), lax.axis_size("row") * 1).astype(jnp.bfloat16),
                    "row",
                    scatter_dimension=0,
                    tiled=True,
                ).astype(jnp.float32)[0]
            )
        rest_blk = pending.astype(jnp.bfloat16)
        answer = jnp.einsum(
            "ba,bn->an", diag_inverse[height, 0, 0], rest_blk, preferred_element_type=jnp.float32
        ).astype(jnp.bfloat16)
        results[height] = answer
        if height > 0:
            spread_x = lax.all_gather(answer[None], "col", axis=0, tiled=True)
            x_rows = lax.dynamic_update_slice_in_dim(x_rows, spread_x, height * columns, 0)
    return jnp.stack(results)[:, None, None]


def shards(load_cases, diag_inverse, factor_tiles, targets, tile_live):
    levels = load_cases.shape[0]
    columns = lax.axis_size("col")
    masked = jnp.where(
        tile_live[:, 0, :, :, None, None] > 0, factor_tiles[:, 0], jnp.zeros((), factor_tiles.dtype)
    )
    offsets = (jnp.arange(1, levels, dtype=jnp.int32) * columns)[:, None, None]
    places = targets[:, 0] + offsets
    return solve_panel(load_cases, diag_inverse, masked, places, tile_live)


def solution(mesh):
    return jax.shard_map(
        shards,
        mesh=mesh,
        in_specs=(
            P(None, "col", "row", None, "rhs"),
            P(None, "col", "row", None, None),
            P(None, "col", None, "row", None, None),
            P(None, "col", None, "row"),
            P(None, "col", None, "row"),
        ),
        out_specs=P(None, "col", "row", None, "rhs"),
        check_vma=False,
    )
```

profile of v0, /device:TPU:0, one launch (start us, length us, event | category | flops | bytes accessed | tf_op | source)
XLA Modules:
  0.0 886.6 jit_solution(6864297268159731490)
XLA Ops:
  6.5 1.8 convolution_convert_fusion.11
  10.4 17.5 %bitcast_select_fusion = bf16[5,16,2,256,256]{4,3,2,1,0:T(8,128)(2,1)} fusion(bf16[5,1,16,2,256,256]{5,4,3,2,1,0:T(8,128)(2,1)} %param.7, pred[5,16,2]{2,1,0:T(8,128)(4,1)S(1)} %copy.66), kind=kLoop, calls=%fused_computation.10 | loop fusion | flops 10485760 | bytes 41943200 | tf_op jit(solution)/shard_map/jit(_where)/select_n | solution.py:78
  27.9 28.9 %all-gather.16.cloned.1.call-done = bf16[4096,256]{1,0:T(8,128)(2,1)} async-done(((bf16[256,256]{1,0:T(8,128)(2,1)}), bf16[4096,256]{1,0:T(8,128)(2,1)}) %all-gather.16.cloned.1.call-update) | async-done | bytes 2097168 | tf_op jit(solution)/shard_map/all_gather | solution.py:45
  56.8 7.4 fusion.1
  64.5 11.8 %scatter_fusion = f32[12,256,256]{2,1,0:T(8,128)S(1)} fusion(f32[12,256,256]{2,1,0:T(8,128)S(1)} %broadcast_in_dim.62, s32[32]{0:T(128)S(1)} %get-tuple-element.15, f32[32,256,256]{2,1,0:T(8,128)} %bitcast.276), kind=kCustom, calls=%fused_computation.5 | custom fusion | flops 2097152 | bytes 25165952 | tf_op jit(solution)/shard_map/scatter-add | solution.py:13
  76.2 0.8 slice.138
  77.1 10.0 %reduce-scatter.21.cloned.1.call-done = f32[1,256,256]{2,1,0:T(8,128)} async-done(((f32[2,256,256]{2,1,0:T(8,128)}), f32[1,256,256]{2,1,0:T(8,128)}) %reduce-scatter.21.cloned.1.call-update) | async-done | bytes 262160 | tf_op jit(solution)/shard_map/reduce_scatter | solution.py:35
  87.1 1.9 fusion.10
  89.1 49.4 %all-gather.18.cloned.1.call-done = bf16[4096,256]{0,1:T(8,128)(2,1)} async-done(((bf16[256,256]{0,1:T(8,128)(2,1)}), bf16[4096,256]{0,1:T(8,128)(2,1)}) %all-gather.18.cloned.1.call-update) | async-done | bytes 2097168 | tf_op jit(solution)/shard_map/all_gather | solution.py:45
  138.5 4.1 copy.111
  142.6 7.4 fusion.3
  150.0 11.7 %scatter_fusion.1 = f32[12,256,256]{2,1,0:T(8,128)S(1)} fusion(f32[12,256,256]{2,1,0:T(8,128)S(1)} %scatter_fusion, s32[32]{0:T(128)S(1)} %get-tuple-element.16, f32[32,256,256]{2,1,0:T(8,128)} %bitcast.277), kind=kCustom, calls=%fused_computation.6 | custom fusion | flops 2097152 | bytes 25165952 | tf_op jit(solution)/shard_map/scatter-add | solution.py:13
  161.7 0.8 slice.141
  162.6 10.0 %reduce-scatter.23.cloned.1.call-done = f32[1,256,256]{2,1,0:T(8,128)} async-done(((f32[2,256,256]{2,1,0:T(8,128)}), f32[1,256,256]{2,1,0:T(8,128)}) %reduce-scatter.23.cloned.1.call-update) | async-done | bytes 262160 | tf_op jit(solution)/shard_map/reduce_scatter | solution.py:35
  172.6 1.9 fusion.11
  175.0 48.8 %all-gather.20.cloned.1.call-done = bf16[4096,256]{0,1:T(8,128)(2,1)} async-done(((bf16[256,256]{0,1:T(8,128)(2,1)}), bf16[4096,256]{0,1:T(8,128)(2,1)}) %all-gather.20.cloned.1.call-update) | async-done | bytes 2097168 | tf_op jit(solution)/shard_map/all_gather | solution.py:45
  223.7 4.1 copy.112
  227.8 7.4 fusion.5
  235.2 11.7 %scatter_fusion.2 = f32[12,256,256]{2,1,0:T(8,128)S(1)} fusion(f32[12,256,256]{2,1,0:T(8,128)S(1)} %scatter_fusion.1, s32[32]{0:T(128)S(1)} %get-tuple-element.17, f32[32,256,256]{2,1,0:T(8,128)} %bitcast.279), kind=kCustom, calls=%fused_computation.7 | custom fusion | flops 2097152 | bytes 25165952 | tf_op jit(solution)/shard_map/scatter-add | solution.py:13
  247.8 10.0 %reduce-scatter.25.cloned.1.call-done = f32[1,256,256]{2,1,0:T(8,128)} async-done(((f32[2,256,256]{2,1,0:T(8,128)}), f32[1,256,256]{2,1,0:T(8,128)}) %reduce-scatter.25.cloned.1.call-update) | async-done | bytes 262160 | tf_op jit(solution)/shard_map/reduce_scatter | solution.py:35
  257.8 1.9 fusion.12
  259.8 49.4 %all-gather.22.cloned.1.call-done = bf16[4096,256]{0,1:T(8,128)(2,1)} async-done(((bf16[256,256]{0,1:T(8,128)(2,1)}), bf16[4096,256]{0,1:T(8,128)(2,1)}) %all-gather.22.cloned.1.call-update) | async-done | bytes 2097168 | tf_op jit(solution)/shard_map/all_gather | solution.py:45
  309.2 4.1 copy.113
  313.3 7.4 fusion.7
  320.7 11.7 %scatter_fusion.3 = f32[12,256,256]{2,1,0:T(8,128)S(1)} fusion(f32[12,256,256]{2,1,0:T(8,128)S(1)} %scatter_fusion.2, s32[32]{0:T(128)S(1)} %get-tuple-element.18, f32[32,256,256]{2,1,0:T(8,128)} %bitcast.278), kind=kCustom, calls=%fused_computation.8 | custom fusion | flops 2097152 | bytes 25165952 | tf_op jit(solution)/shard_map/scatter-add | solution.py:13
  333.4 9.8 %reduce-scatter.27.cloned.1.call-done = f32[1,256,256]{2,1,0:T(8,128)} async-done(((f32[2,256,256]{2,1,0:T(8,128)}), f32[1,256,256]{2,1,0:T(8,128)}) %reduce-scatter.27.cloned.1.call-update) | async-done | bytes 262160 | tf_op jit(solution)/shard_map/reduce_scatter | solution.py:35
  343.2 1.9 fusion.13
  345.4 49.0 %all-gather.24.cloned.1.call-done = bf16[4096,256]{0,1:T(8,128)(2,1)} async-done(((bf16[256,256]{0,1:T(8,128)(2,1)}), bf16[4096,256]{0,1:T(8,128)(2,1)}) %all-gather.24.cloned.1.call-update) | async-done | bytes 2097168 | tf_op jit(solution)/shard_map/all_gather | solution.py:45
  394.4 4.1 copy.114
  398.5 7.4 fusion.9
  405.9 11.6 %scatter_fusion.4 = f32[12,256,256]{2,1,0:T(8,128)S(1)} fusion(f32[12,256,256]{2,1,0:T(8,128)S(1)} %scatter_fusion.3, s32[32]{0:T(128)S(1)} %fusion.89, f32[32,256,256]{2,1,0:T(8,128)} %bitcast.280), kind=kCustom, calls=%fused_computation.9 | custom fusion | flops 2097152 | bytes 25165952 | tf_op jit(solution)/shard_map/scatter-add | solution.py:13
  418.6 9.8 %reduce-scatter.29.cloned.1.call-done = f32[1,256,256]{2,1,0:T(8,128)} async-done(((f32[2,256,256]{2,1,0:T(8,128)}), f32[1,256,256]{2,1,0:T(8,128)}) %reduce-scatter.29.cloned.1.call-update) | async-done | bytes 262160 | tf_op jit(solution)/shard_map/reduce_scatter | solution.py:35
  428.3 1.5 convolution_convert_fusion.5
  429.8 2.1 all-gather.5
  432.2 2.8 gather_fusion
  435.0 6.2 bitcast_convert_fusion.4
  441.1 4.0 copy.79
  445.6 75.4 %reduce-scatter.31.cloned.1.call-done = bf16[1,256,256]{1,2,0:T(8,128)(2,1)} async-done(((bf16[16,256,256]{1,2,0:T(8,128)(2,1)}), bf16[1,256,256]{1,2,0:T(8,128)(2,1)}) %reduce-scatter.31.cloned.1.call-update) | async-done | bytes 131088
  521.0 1.1 convolution_convert_fusion.4
  522.0 2.0 all-gather.6
  524.2 2.8 gather_fusion.1
  527.0 6.2 bitcast_convert_fusion.3
  533.2 3.9 copy.83
  537.2 73.6 %reduce-scatter.33.cloned.1.call-done = bf16[1,256,256]{1,2,0:T(8,128)(2,1)} async-done(((bf16[16,256,256]{1,2,0:T(8,128)(2,1)}), bf16[1,256,256]{1,2,0:T(8,128)(2,1)}) %reduce-scatter.33.cloned.1.call-update) | async-done | bytes 131088
  610.8 1.1 convolution_convert_fusion.3
  611.9 2.0 all-gather.7
  614.0 2.8 gather_fusion.2
  616.8 6.2 bitcast_convert_fusion.2
  623.0 3.9 copy.87
  627.4 73.3 %reduce-scatter.35.cloned.1.call-done = bf16[1,256,256]{1,2,0:T(8,128)(2,1)} async-done(((bf16[16,256,256]{1,2,0:T(8,128)(2,1)}), bf16[1,256,256]{1,2,0:T(8,128)(2,1)}) %reduce-scatter.35.cloned.1.call-update) | async-done | bytes 131088
  700.7 1.1 convolution_convert_fusion.2
  701.8 2.2 all-gather.8
  704.1 2.8 gather_fusion.3
  706.9 6.2 bitcast_convert_fusion.1
  713.1 3.9 copy.91
  717.1 73.6 %reduce-scatter.37.cloned.1.call-done = bf16[1,256,256]{1,2,0:T(8,128)(2,1)} async-done(((bf16[16,256,256]{1,2,0:T(8,128)(2,1)}), bf16[1,256,256]{1,2,0:T(8,128)(2,1)}) %reduce-scatter.37.cloned.1.call-update) | async-done | bytes 131088
  790.7 1.1 convolution_convert_fusion.1
  791.8 2.1 all-gather.9
  793.9 1.1 copy.119
  795.0 2.8 gather_fusion.4
  797.8 6.2 bitcast_convert_fusion
  804.1 73.6 %reduce-scatter.39.cloned.1.call-done = bf16[1,256,256]{2,1,0:T(8,128)(2,1)} async-done(((bf16[16,256,256]{2,1,0:T(8,128)(2,1)}), bf16[1,256,256]{2,1,0:T(8,128)(2,1)}) %reduce-scatter.39.cloned.1.call-update) | async-done | bytes 131088
  877.7 1.1 fusion.15
  878.9 1.2 copy.95
  (92 shorter events, 7.9 us)
Async XLA Ops:
  6.5 50.3 %all-gather.16.cloned.1.call-start = ((), (), s32[]{:S(2)}) async-start(), calls=%async_computation.15 | async-start | bytes 2228224 | tf_op jit(solution)/shard_map/all_gather | solution.py:45
  8.4 78.7 %reduce-scatter.21.cloned.1.call-start = ((), (), s32[]{:S(2)}) async-start(), calls=%async_computation.10 | async-start | bytes 786432 | tf_op jit(solution)/shard_map/reduce_scatter | solution.py:35
  77.1 61.4 %all-gather.18.cloned.1.call-start = ((), (), s32[]{:S(2)}) async-start(), calls=%async_computation.16 | async-start | bytes 2228224 | tf_op jit(solution)/shard_map/all_gather | solution.py:45
  89.1 83.5 %reduce-scatter.23.cloned.1.call-start = ((), (), s32[]{:S(2)}) async-start(), calls=%async_computation.11 | async-start | bytes 786432 | tf_op jit(solution)/shard_map/reduce_scatter | solution.py:35
  162.6 61.2 %all-gather.20.cloned.1.call-start = ((), (), s32[]{:S(2)}) async-start(), calls=%async_computation.17 | async-start | bytes 2228224 | tf_op jit(solution)/shard_map/all_gather | solution.py:45
  174.6 83.2 %reduce-scatter.25.cloned.1.call-start = ((), (), s32[]{:S(2)}) async-start(), calls=%async_computation.12 | async-start | bytes 786432 | tf_op jit(solution)/shard_map/reduce_scatter | solution.py:35
  247.8 61.5 %all-gather.22.cloned.1.call-start = ((), (), s32[]{:S(2)}) async-start(), calls=%async_computation.18 | async-start | bytes 2228224 | tf_op jit(solution)/shard_map/all_gather | solution.py:45
  259.8 83.5 %reduce-scatter.27.cloned.1.call-start = ((), (), s32[]{:S(2)}) async-start(), calls=%async_computation.13 | async-start | bytes 786432 | tf_op jit(solution)/shard_map/reduce_scatter | solution.py:35
  333.2 61.2 %all-gather.24.cloned.1.call-start = ((), (), s32[]{:S(2)}) async-start(), calls=%async_computation.19 | async-start | bytes 2228224 | tf_op jit(solution)/shard_map/all_gather | solution.py:45
  345.2 83.2 %reduce-scatter.29.cloned.1.call-start = ((), (), s32[]{:S(2)}) async-start(), calls=%async_computation.14 | async-start | bytes 786432 | tf_op jit(solution)/shard_map/reduce_scatter | solution.py:35
  418.3 102.6 %reduce-scatter.31.cloned.1.call-start = ((), (), s32[]{:S(2)}) async-start(), calls=%async_computation.20 | async-start | bytes 2228224
  441.1 79.8 %copy-start = (bf16[6,1,1,256,256]{4,3,2,1,0:T(8,128)(2,1)S(1)}, bf16[6,1,1,256,256]{4,3,2,1,0:T(8,128)(2,1)}, u32[]{:S(2)}) copy-start(bf16[6,1,1,256,256]{4,3,2,1,0:T(8,128)(2,1)} %param.6) | copy-start | bytes 2359300
  441.1 79.8 %copy-start.4 = (bf16[256,256]{0,1:T(8,128)(2,1)S(1)}, bf16[256,256]{0,1:T(8,128)(2,1)}, u32[]{:S(2)}) copy-start(bf16[256,256]{0,1:T(8,128)(2,1)} %fusion.13) | copy-start | bytes 393220
  445.1 165.6 %reduce-scatter.33.cloned.1.call-start = ((), (), s32[]{:S(2)}) async-start(), calls=%async_computation.21 | async-start | bytes 2228224
  533.2 77.6 %copy-start.3 = (bf16[256,256]{0,1:T(8,128)(2,1)S(1)}, bf16[256,256]{0,1:T(8,128)(2,1)}, u32[]{:S(2)}) copy-start(bf16[256,256]{0,1:T(8,128)(2,1)} %fusion.12) | copy-start | bytes 393220
  537.1 163.5 %reduce-scatter.35.cloned.1.call-start = ((), (), s32[]{:S(2)}) async-start(), calls=%async_computation.22 | async-start | bytes 2228224
  623.0 77.7 %copy-start.2 = (bf16[256,256]{0,1:T(8,128)(2,1)S(1)}, bf16[256,256]{0,1:T(8,128)(2,1)}, u32[]{:S(2)}) copy-start(bf16[256,256]{0,1:T(8,128)(2,1)} %fusion.11) | copy-start | bytes 393220
  626.9 163.8 %reduce-scatter.37.cloned.1.call-start = ((), (), s32[]{:S(2)}) async-start(), calls=%async_computation.23 | async-start | bytes 2228224
  713.1 77.6 %copy-start.1 = (bf16[256,256]{0,1:T(8,128)(2,1)S(1)}, bf16[256,256]{0,1:T(8,128)(2,1)}, u32[]{:S(2)}) copy-start(bf16[256,256]{0,1:T(8,128)(2,1)} %fusion.10) | copy-start | bytes 393220
  717.0 160.7 %reduce-scatter.39.cloned.1.call-start = ((), (), s32[]{:S(2)}) async-start(), calls=%async_computation.24 | async-start | bytes 2228224
  797.8 79.9 %copy-start.5 = (bf16[256,256]{1,0:T(8,128)(2,1)S(1)}, bf16[256,256]{1,0:T(8,128)(2,1)}, u32[]{:S(2)}) copy-start(bf16[256,256]{1,0:T(8,128)(2,1)} %convolution_convert_fusion.11) | copy-start | bytes 393220
Sparse Core Ops, SparseCore 0:
  9.5 47.2 all-gather.15
  77.2 9.8 reduce-scatter.20
  89.5 49.0 all-gather.17
  162.7 9.8 reduce-scatter.22
  174.7 49.0 all-gather.19
  247.9 9.8 reduce-scatter.24
  260.1 49.0 all-gather.21
  333.3 9.8 reduce-scatter.26
  345.4 49.0 all-gather.23
  418.4 9.8 reduce-scatter.28
  445.3 75.6 reduce-scatter.30
  537.2 73.4 reduce-scatter.32
  627.1 73.5 reduce-scatter.34
  717.2 73.4 reduce-scatter.36
  804.2 73.4 reduce-scatter.38
where the time goes:
time: 888 us; the launch traced here: 887 us
  waiting for transfers between devices  645 us (73%)
  matrix products  84.3 us (9%)
  other arithmetic  77.4 us (9%)
  local copies, waits for them, and re-layouts  55.2 us (6%)
  between operations  13.6 us (2%)
  blocking collectives  10.4 us (1%)
    unnamed x20, waiting for transfers between devices  370 us
    all_gather x5, waiting for transfers between devices, solve_panel(): lax.all_gather(solved_blk[None], 'row', axis=0, tiled=True)  225 us
    scatter-add x5, other arithmetic, add_updates(): partials.at[places_level.reshape(-1)]  58.5 us
    reduce_scatter x5, waiting for transfers between devices, solve_panel(): lax.psum_scatter(pending_rows, 'col', scatter_dimension=0, tiled=True)[0]  49.6 us
    dot_general x5, matrix products, add_updates(): jnp.einsum('qkab,qbn->qkan', tiles_level, shard_piece, preferred_element_...  37 us
    dot_general x5, matrix products, back_terms(): jnp.einsum('qkab,qkan->qbn', tiles_level, gathered, preferred_element_typ...  30.9 us
  transfers between devices with their start and end apart: 15, of which 15 were waited for; matrix products, arithmetic and copies ran while one was open for 2% of the time, Pallas kernels for 0%

commit v1 on v0

v1 whole, which is shorter than its diff:
```python
from functools import partial

import jax
import jax.numpy as jnp
import numpy as np
from jax import lax
from jax.experimental import pallas as pl
from jax.experimental.pallas import tpu as pltpu
from jax.sharding import Mesh, PartitionSpec as P

F32, BF16 = jnp.float32, jnp.bfloat16
AXES = ("y", "x", "col")
SHIFTS = (0, 1, 3, 2)
VMEM = pl.BlockSpec(memory_space=pltpu.VMEM)
SMEM = pl.BlockSpec(memory_space=pltpu.SMEM)
ANY = pl.BlockSpec(memory_space=pl.ANY)


def pairs(near, shift):
    out = []
    for y in range(4):
        for x in range(4):
            for c in range(2):
                on_x = (c == 0) == near
                ty, tx = (y, (x + shift) % 4) if on_x else ((y + shift) % 4, x)
                out.append(((y * 4 + x) * 2 + c, (ty * 4 + tx) * 2 + c))
    return out


def send(value, near, shift):
    return lax.ppermute(value, AXES, pairs(near, shift))


def swap_cores(value):
    return lax.ppermute(value, "col", [(0, 1), (1, 0)])


def call(body, out, in_specs, out_specs, scratch=(), aliases={}, flops=0, moved=0, limit=16):
    return pl.pallas_call(
        body,
        out_shape=out,
        in_specs=in_specs,
        out_specs=out_specs,
        scratch_shapes=list(scratch),
        input_output_aliases=aliases,
        compiler_params=pltpu.CompilerParams(vmem_limit_bytes=limit << 20),
        cost_estimate=pl.CostEstimate(flops=flops, bytes_accessed=moved, transcendentals=0),
    )


def dot(a, b):
    return jnp.dot(a, b, preferred_element_type=F32)


def fetch(tiles, level, order, first, count, buf, sems):
    copies = [
        pltpu.make_async_copy(tiles.at[level, 0, order[first + i]], buf.at[i], sems.at[i])
        for i in range(count)
    ]
    for copy in copies:
        copy.start()
    return copies


def fold_body(level, first, groups, zero, finish, *refs):
    refs = list(refs)
    order, places = refs[:2]
    blocks = refs[2 : 2 + groups]
    refs = refs[2 + groups :]
    tiles = refs.pop(0)
    if not zero:
        refs.pop(0)
    load = refs.pop(0) if finish else None
    acc = refs.pop(0)
    if finish:
        pending, outgoing = refs.pop(0), refs.pop(0)
    buf, sems = refs
    count = 4 * groups
    copies = fetch(tiles, level, order, first, count, buf, sems)
    if zero:
        acc[...] = jnp.zeros_like(acc)
    size = acc.shape[1]
    for i in range(count):
        copies[i].wait()
        product = dot(buf[i].reshape(2 * size, size), blocks[i // 4][i % 4])
        for k in range(2):
            place = places[level, first + i, k]
            acc[place] += product[k * size : (k + 1) * size]
    if finish:
        pending[...] = load[...].astype(F32) - acc[2 * level]
        outgoing[...] = acc[2 * level + 1]


def fold(level, first, order, places, blocks, tiles, acc, load=None):
    groups = len(blocks)
    size, cases = blocks[0].shape[1:]
    levels = tiles.shape[0]
    count = 4 * groups
    zero, finish = acc is None, load is not None
    out = [jax.ShapeDtypeStruct((2 * levels + 1, size, cases), F32)]
    args = [order, places, *blocks, tiles]
    specs = [SMEM, SMEM] + [VMEM] * groups + [ANY]
    aliases = {}
    if not zero:
        aliases = {len(args): 0}
        args.append(acc)
        specs.append(VMEM)
    if finish:
        args.append(load)
        specs.append(VMEM)
        out += [jax.ShapeDtypeStruct((size, cases), F32)] * 2
    return call(
        partial(fold_body, level, first, groups, zero, finish),
        out,
        specs,
        [VMEM] * len(out),
        [pltpu.VMEM((count, 2, size, size), BF16), pltpu.SemaphoreType.DMA((count,))],
        aliases,
        flops=count * 4 * size * size * cases,
        moved=count * 4 * size * size,
    )(*args)


def solve_body(pending, received, inverse, solved):
    solved[...] = dot(inverse[...], (pending[...] - received[...]).astype(BF16)).astype(BF16)


def solve(pending, received, inverse):
    return call(
        solve_body, jax.ShapeDtypeStruct(pending.shape, BF16), [VMEM] * 3, VMEM, limit=8, flops=1 << 25, moved=1 << 20
    )(pending, received, inverse)


def back_body(level, first, groups, order, places, x_rows, tiles, *refs):
    outs = refs[:groups]
    buf, sems = refs[groups:]
    count = 4 * groups
    copies = fetch(tiles, level, order, first, count, buf, sems)
    for i in range(count):
        copies[i].wait()
        total = dot(x_rows[places[level, first + i, 0]], buf[i, 0])
        total += dot(x_rows[places[level, first + i, 1]], buf[i, 1])
        outs[i // 4][i % 4] = total.astype(BF16)


def back(level, first, groups, order, places, x_rows, tiles):
    cases, size = x_rows.shape[1:]
    count = 4 * groups
    return call(
        partial(back_body, level, first, groups),
        [jax.ShapeDtypeStruct((4, cases, size), BF16)] * groups,
        [SMEM, SMEM, VMEM, ANY],
        [VMEM] * groups,
        [pltpu.VMEM((count, 2, size, size), BF16), pltpu.SemaphoreType.DMA((count,))],
        flops=count * 4 * size * size * cases,
        moved=count * 4 * size * size,
    )(order, places, x_rows, tiles)


def add_body(a, b, c, d, out):
    for i in range(4):
        total = a[i].astype(F32) + b[i].astype(F32) + c[i].astype(F32) + d[i].astype(F32)
        out[i] = total.astype(BF16)


def add_four(parts):
    shape = jax.ShapeDtypeStruct(parts[0].shape, BF16)
    return call(add_body, shape, [VMEM] * 4, VMEM, limit=8, flops=1 << 20, moved=1 << 21)(*parts)


def answer_body(solved, own, a, b, c, inverse, out):
    term = own[0].astype(F32) + a[...].astype(F32) + b[...].astype(F32) + c[...].astype(F32)
    out[...] = dot((solved[...].astype(F32) - term).astype(BF16), inverse[...]).astype(BF16)


def answer(solved, own, received, inverse):
    shape = jax.ShapeDtypeStruct(solved.shape, BF16)
    return call(answer_body, shape, [VMEM] * 6, VMEM, limit=8, flops=1 << 25, moved=1 << 20)(
        solved, own, *received, inverse
    )


def shards(load_cases, diag_inverse, factor_tiles, targets, tile_live):
    levels = load_cases.shape[0]
    size, cases = load_cases.shape[3:]
    y, x, c = (lax.axis_index(name) for name in AXES)
    shifts = jnp.array(SHIFTS, jnp.int32)
    far, near = shifts[:, None], shifts[None, :]

    def order_of(sign):
        ys = jnp.where(c == 0, y + sign * far + 0 * near, y + sign * near + 0 * far) % 4
        xs = jnp.where(c == 0, x + sign * near + 0 * far, x + sign * far + 0 * near) % 4
        return (ys * 4 + xs).reshape(-1)

    level_ids = jnp.arange(levels - 1, dtype=jnp.int32)[:, None, None]
    owner = targets[:, 0]
    places = 2 * (level_ids + owner // 2) + ((owner % 2) ^ c)
    places = jnp.where(tile_live[:, 0] > 0, places, 2 * (levels - 1))
    order_in, order_out = order_of(-1), order_of(1)
    places_in, places_out = places[:, order_in], places[:, order_out]
    inverse = [diag_inverse[h, 0, 0] for h in range(levels)]
    load = [load_cases[h, 0, 0] for h in range(levels)]

    solved = [dot(inverse[0], load[0]).astype(BF16)]
    acc = None
    for height in range(levels - 1):
        mine = solved[height]
        group = jnp.stack([mine] + [send(mine, True, s) for s in SHIFTS[1:]])
        far_groups = [send(group, False, s) for s in SHIFTS[1:]]
        (acc,) = fold(height, 0, order_in, places_in, [group], factor_tiles, acc)
        acc, pending, outgoing = fold(
            height, 4, order_in, places_in, far_groups, factor_tiles, acc, load[height + 1]
        )
        solved.append(solve(pending, swap_cores(outgoing), inverse[height + 1]))

    results = [None] * levels
    x_rows = jnp.zeros((2 * levels - 1, cases, size), BF16)
    latest = lax.dot_general(
        solved[-1], inverse[-1], (((0,), (0,)), ((), ())), preferred_element_type=F32
    ).astype(BF16)
    results[-1] = latest.T
    for height in reversed(range(levels - 1)):
        x_rows = x_rows.at[2 * height].set(latest).at[2 * height + 1].set(swap_cores(latest))
        parts = back(height, 4, 3, order_out, places_out, x_rows, factor_tiles)
        moved = [send(part, False, s) for part, s in zip(parts, SHIFTS[1:])]
        (kept,) = back(height, 0, 1, order_out, places_out, x_rows, factor_tiles)
        group = add_four([kept] + moved)
        received = [send(group[i], True, SHIFTS[i]) for i in range(1, 4)]
        latest = answer(solved[height].T, group, received, inverse[height])
        results[height] = latest.T
    return jnp.stack(results)[:, None, None]


def solution(mesh):
    devices = mesh.devices
    split = Mesh(devices.reshape((4, 4) + devices.shape[1:]), ("y", "x", "col", "rhs"))
    row = ("y", "x")
    return jax.shard_map(
        shards,
        mesh=split,
        in_specs=(
            P(None, "col", row, None, "rhs"),
            P(None, "col", row, None, None),
            P(None, "col", None, row, None, None),
            P(None, "col", None, row),
            P(None, "col", None, row),
        ),
        out_specs=P(None, "col", row, None, "rhs"),
        check_vma=False,
    )
```

time: 888 us -> 402 us (0.45)
  waiting for transfers between devices: 645 us -> 155 us
  matrix products: 84.3 us -> 2.4 us
  Pallas kernels: 0 us -> 79.3 us
  starting transfers between devices: 0.77 us -> 79.8 us
  other arithmetic: 77.4 us -> 2.22 us
  local copies, waits for them, and re-layouts: 55.2 us -> 74.1 us
  between operations: 13.6 us -> 1.38 us
  blocking collectives: 10.4 us -> 0 us
    unnamed x20 -> x0, waiting for transfers between devices: 370 us -> none
    all_gather x5 -> x0, waiting for transfers between devices: 225 us -> none  [solve_panel(): lax.all_gather(solved_blk[None], 'row', axis=0, tiled=True)]
    ppermute x0 -> x70, waiting for transfers between devices: none -> 155 us  [the longest x60 142 us: send(): return lax.ppermute(value, AXES, pairs(near, shift))]
    dot_general x21 -> x2, matrix products: 84.3 us -> 2.4 us  [the longest x1 1.26 us: dot(): return jnp.dot(a, b, preferred_element_type=F32)]
    ppermute x0 -> x70, starting transfers between devices: none -> 79.8 us  [the longest x60 78.2 us: send(): return lax.ppermute(value, AXES, pairs(near, shift))]
    pallas_call x0 -> x35, Pallas kernels: none -> 79.3 us  [the longest x10 38.4 us: fold(): call(partial(fold_body, level, first, groups, zero, finish), out, specs,...]
    unnamed x16 -> x81, local copies, waits for them, and re-layouts: 0.07 us -> 60.4 us
    scatter-add x5 -> x0, other arithmetic: 58.5 us -> none  [add_updates(): partials.at[places_level.reshape(-1)]]
  transfers between devices with their start and end apart: 15 -> 70, of which waited for: 15 -> 62; matrix products, arithmetic and copies ran while one was open for 2% -> 3% of each run, Pallas kernels for 0% -> 6%
where the time goes in v1:
time: 402 us; the launch traced here: 394 us
  waiting for transfers between devices  155 us (39%)
  starting transfers between devices  79.8 us (20%)
  Pallas kernels  79.3 us (20%)
  local copies, waits for them, and re-layouts  74.1 us (18%)
    ppermute x60, waiting for transfers between devices, send(): return lax.ppermute(value, AXES, pairs(near, shift))  142 us
    ppermute x60, starting transfers between devices, send(): return lax.ppermute(value, AXES, pairs(near, shift))  78.2 us
    unnamed x81, local copies, waits for them, and re-layouts  60.4 us
    pallas_call x10, Pallas kernels, fold(): call(partial(fold_body, level, first, groups, zero, finish), out, specs,...  38.4 us
    pallas_call x10, Pallas kernels, back(): call(partial(back_body, level, first, groups), [jax.ShapeDtypeStruct((4,...  37.6 us
    ppermute x10, waiting for transfers between devices, swap_cores(): return lax.ppermute(value, 'col', [(0, 1), (1, 0)])  12.6 us
  transfers between devices with their start and end apart: 70, of which 62 were waited for; matrix products, arithmetic and copies ran while one was open for 3% of the time, Pallas kernels for 6%

profile of v1, /device:TPU:0, one launch (start us, length us, event | category | flops | bytes accessed | tf_op | source)
XLA Modules:
  0.0 394.2 jit_solution(3546659328145535753)
XLA Ops:
  20.4 7.0 %copy-done = bf16[5,1,16,2,256,256]{5,4,3,2,1,0:T(8,128)(2,1)S(1)} copy-done((bf16[5,1,16,2,256,256]{5,4,3,2,1,0:T(8,128)(2,1)S(1)}, bf16[5,1,16,2,256,256]{5,4,3,2,1,0:T(8,128)(2,1)}, u32[]{:S(2)}) %copy-start) | copy-done | bytes 20971544
  27.3 2.7 shard_map.64.refs_6_
  35.4 7.0 %copy-done.1 = bf16[5,1,16,2,256,256]{5,4,3,2,1,0:T(8,128)(2,1)S(1)} copy-done((bf16[5,1,16,2,256,256]{5,4,3,2,1,0:T(8,128)(2,1)S(1)}, bf16[5,1,16,2,256,256]{5,4,3,2,1,0:T(8,128)(2,1)}, u32[]{:S(2)}) %copy-start.1) | copy-done | bytes 20971544
  45.3 5.0 %shard_map.65 = (f32[11,256,256]{2,1,0:T(8,128)S(1)}, f32[256,256]{1,0:T(8,128)S(1)}, f32[256,256]{1,0:T(8,128)S(1)}) custom-call(s32[16]{0:T(128)S(1)} %fusion.7.refs_0_, s32[5,16,2]{2,1,0:T(8,128)S(1)} %bitcast.150, bf16[4,256,256]{2,1,0:T(8,128)(2,1)S(1)} %copy.32.refs_2_, bf16[4,256,256]{2,1,0:T(8,128)(2,1)S(1)} %copy-done.8, ...), custom_call_target="tpu_custom_call", output_to_operand_aliasing={{0}: (6, {})} | custom-call | flops 805306368 | bytes 3145728 | tf_op jit(solution)/shard_map/pallas_call | solution.py:112
  52.5 3.0 collective-permute-start.8
  59.4 2.5 collective-permute-done.9
  62.7 2.6 collective-permute-start.11
  68.2 9.9 %collective-permute-done.10.refs_2_ = bf16[4,256,256]{2,1,0:T(8,128)(2,1)S(1)} collective-permute-done((bf16[4,256,256]{2,1,0:T(8,128)(2,1)S(1)}, bf16[4,256,256]{2,1,0:T(8,128)(2,1)S(1)}, u32[]{:S(2)}, u32[]{:S(2)}) %collective-permute-start.10) | collective-permute-done | bytes 524320 | tf_op jit(solution)/shard_map/ppermute | solution.py:31
  78.1 5.0 %shard_map.68 = (f32[11,256,256]{2,1,0:T(8,128)S(1)}, f32[256,256]{1,0:T(8,128)S(1)}, f32[256,256]{1,0:T(8,128)S(1)}) custom-call(s32[16]{0:T(128)S(1)} %fusion.7.refs_0_, s32[5,16,2]{2,1,0:T(8,128)S(1)} %bitcast.152, bf16[4,256,256]{2,1,0:T(8,128)(2,1)S(1)} %collective-permute-done.10.refs_2_, ...), custom_call_target="tpu_custom_call", output_to_operand_aliasing={{0}: (6, {})} | custom-call | flops 805306368 | bytes 3145728 | tf_op jit(solution)/shard_map/pallas_call | solution.py:112
  85.0 3.2 collective-permute-start.15
  88.2 2.9 collective-permute-done.14
  92.2 2.5 collective-permute-done.16
  102.0 3.2 collective-permute-done.17.refs_2_
  105.2 5.3 %collective-permute-done.18.refs_3_ = bf16[4,256,256]{2,1,0:T(8,128)(2,1)S(1)} collective-permute-done((bf16[4,256,256]{2,1,0:T(8,128)(2,1)S(1)}, bf16[4,256,256]{2,1,0:T(8,128)(2,1)S(1)}, u32[]{:S(2)}, u32[]{:S(2)}) %collective-permute-start.18) | collective-permute-done | bytes 524320 | tf_op jit(solution)/shard_map/ppermute | solution.py:31
  112.3 5.0 %shard_map.71 = (f32[11,256,256]{2,1,0:T(8,128)S(1)}, f32[256,256]{1,0:T(8,128)S(1)}, f32[256,256]{1,0:T(8,128)S(1)}) custom-call(s32[16]{0:T(128)S(1)} %fusion.7.refs_0_, s32[5,16,2]{2,1,0:T(8,128)S(1)} %bitcast.154, bf16[4,256,256]{2,1,0:T(8,128)(2,1)S(1)} %collective-permute-done.17.refs_2_, ...), custom_call_target="tpu_custom_call", output_to_operand_aliasing={{0}: (6, {})} | custom-call | flops 805306368 | bytes 3145728 | tf_op jit(solution)/shard_map/pallas_call | solution.py:112
  119.2 3.2 collective-permute-start.22
  122.4 2.9 collective-permute-done.21
  126.4 2.5 collective-permute-done.23
  135.5 4.0 %collective-permute-done.24.refs_2_ = bf16[4,256,256]{2,1,0:T(8,128)(2,1)S(1)} collective-permute-done((bf16[4,256,256]{2,1,0:T(8,128)(2,1)S(1)}, bf16[4,256,256]{2,1,0:T(8,128)(2,1)S(1)}, u32[]{:S(2)}, u32[]{:S(2)}) %collective-permute-start.24) | collective-permute-done | bytes 524320 | tf_op jit(solution)/shard_map/ppermute | solution.py:31
  139.4 5.2 %collective-permute-done.25.refs_3_ = bf16[4,256,256]{2,1,0:T(8,128)(2,1)S(1)} collective-permute-done((bf16[4,256,256]{2,1,0:T(8,128)(2,1)S(1)}, bf16[4,256,256]{2,1,0:T(8,128)(2,1)S(1)}, u32[]{:S(2)}, u32[]{:S(2)}) %collective-permute-start.25) | collective-permute-done | bytes 524320 | tf_op jit(solution)/shard_map/ppermute | solution.py:31
  145.2 5.0 %shard_map.74 = (f32[11,256,256]{2,1,0:T(8,128)S(1)}, f32[256,256]{1,0:T(8,128)S(1)}, f32[256,256]{1,0:T(8,128)S(1)}) custom-call(s32[16]{0:T(128)S(1)} %fusion.7.refs_0_, s32[5,16,2]{2,1,0:T(8,128)S(1)} %bitcast.156, bf16[4,256,256]{2,1,0:T(8,128)(2,1)S(1)} %collective-permute-done.24.refs_2_, ...), custom_call_target="tpu_custom_call", output_to_operand_aliasing={{0}: (6, {})} | custom-call | flops 805306368 | bytes 3145728 | tf_op jit(solution)/shard_map/pallas_call | solution.py:112
  152.1 3.2 collective-permute-start.29
  155.3 2.9 collective-permute-done.28
  159.2 2.5 collective-permute-done.30
  167.0 7.0 %copy-done.2 = bf16[5,1,16,2,256,256]{5,4,3,2,1,0:T(8,128)(2,1)S(1)} copy-done((bf16[5,1,16,2,256,256]{5,4,3,2,1,0:T(8,128)(2,1)S(1)}, bf16[5,1,16,2,256,256]{5,4,3,2,1,0:T(8,128)(2,1)}, u32[]{:S(2)}) %copy-start.2) | copy-done | bytes 20971544
  179.4 5.9 %shard_map.77 = (f32[11,256,256]{2,1,0:T(8,128)S(1)}, f32[256,256]{1,0:T(8,128)S(1)}, f32[256,256]{1,0:T(8,128)}) custom-call(s32[16]{0:T(128)S(1)} %fusion.7.refs_0_, s32[5,16,2]{2,1,0:T(8,128)S(1)} %bitcast.158, bf16[4,256,256]{2,1,0:T(8,128)(2,1)} %collective-permute-done.31.refs_2_, ...), custom_call_target="tpu_custom_call", output_to_operand_aliasing={{0}: (6, {})} | custom-call | flops 805306368 | bytes 3145728 | tf_op jit(solution)/shard_map/pallas_call | solution.py:112
  190.1 7.0 %copy-done.3 = bf16[5,1,16,2,256,256]{5,4,3,2,1,0:T(8,128)(2,1)S(1)} copy-done((bf16[5,1,16,2,256,256]{5,4,3,2,1,0:T(8,128)(2,1)S(1)}, bf16[5,1,16,2,256,256]{5,4,3,2,1,0:T(8,128)(2,1)}, u32[]{:S(2)}) %copy-start.3) | copy-done | bytes 20971544
  197.1 5.0 %shard_map.80 = (bf16[4,256,256]{2,1,0:T(8,128)(2,1)S(1)}, bf16[4,256,256]{2,1,0:T(8,128)(2,1)S(1)}, bf16[4,256,256]{2,1,0:T(8,128)(2,1)S(1)}) custom-call(s32[16]{0:T(128)S(1)} %fusion.5.order, s32[5,16,2]{2,1,0:T(8,128)S(1)} %bitcast.159, bf16[11,256,256]{2,1,0:T(8,128)(2,1)S(1)} %bitcast_dynamic-update-slice_fusion.14.x_rows, ...), custom_call_target="tpu_custom_call" | custom-call | flops 805306368 | bytes 3145728 | tf_op jit(solution)/shard_map/pallas_call | solution.py:149
  205.8 2.5 shard_map.79.a
  208.3 4.3 %collective-permute-done.36.b = bf16[4,256,256]{2,1,0:T(8,128)(2,1)S(1)} collective-permute-done((bf16[4,256,256]{2,1,0:T(8,128)(2,1)S(1)}, bf16[4,256,256]{2,1,0:T(8,128)(2,1)S(1)}, u32[]{:S(2)}, u32[]{:S(2)}) %collective-permute-start.36) | collective-permute-done | bytes 524320 | tf_op jit(solution)/shard_map/ppermute | solution.py:31
  212.6 5.2 %collective-permute-done.37.c = bf16[4,256,256]{2,1,0:T(8,128)(2,1)S(1)} collective-permute-done((bf16[4,256,256]{2,1,0:T(8,128)(2,1)S(1)}, bf16[4,256,256]{2,1,0:T(8,128)(2,1)S(1)}, u32[]{:S(2)}, u32[]{:S(2)}) %collective-permute-start.37) | collective-permute-done | bytes 524320 | tf_op jit(solution)/shard_map/ppermute | solution.py:31
  218.7 3.2 collective-permute-start.40
  222.0 2.8 collective-permute-done.39.a
  225.8 2.5 collective-permute-done.41.c
  230.1 7.0 %copy-done.4 = bf16[5,1,16,2,256,256]{5,4,3,2,1,0:T(8,128)(2,1)S(1)} copy-done((bf16[5,1,16,2,256,256]{5,4,3,2,1,0:T(8,128)(2,1)S(1)}, bf16[5,1,16,2,256,256]{5,4,3,2,1,0:T(8,128)(2,1)}, u32[]{:S(2)}) %copy-start.4) | copy-done | bytes 20971544
  237.0 5.0 %shard_map.84 = (bf16[4,256,256]{2,1,0:T(8,128)(2,1)S(1)}, bf16[4,256,256]{2,1,0:T(8,128)(2,1)S(1)}, bf16[4,256,256]{2,1,0:T(8,128)(2,1)S(1)}) custom-call(s32[16]{0:T(128)S(1)} %fusion.5.order, s32[5,16,2]{2,1,0:T(8,128)S(1)} %bitcast.161, bf16[11,256,256]{2,1,0:T(8,128)(2,1)S(1)} %bitcast_dynamic-update-slice_fusion.12.x_rows, ...), custom_call_target="tpu_custom_call" | custom-call | flops 805306368 | bytes 3145728 | tf_op jit(solution)/shard_map/pallas_call | solution.py:149
  246.7 2.5 shard_map.83.a
  249.2 3.3 collective-permute-done.43.b
  252.5 5.2 %collective-permute-done.44.c = bf16[4,256,256]{2,1,0:T(8,128)(2,1)S(1)} collective-permute-done((bf16[4,256,256]{2,1,0:T(8,128)(2,1)S(1)}, bf16[4,256,256]{2,1,0:T(8,128)(2,1)S(1)}, u32[]{:S(2)}, u32[]{:S(2)}) %collective-permute-start.44) | collective-permute-done | bytes 524320 | tf_op jit(solution)/shard_map/ppermute | solution.py:31
  259.9 3.2 collective-permute-start.47
  263.2 2.8 collective-permute-done.46.a
  267.0 2.5 collective-permute-done.48.c
  271.5 7.0 %copy-done.5 = bf16[5,1,16,2,256,256]{5,4,3,2,1,0:T(8,128)(2,1)S(1)} copy-done((bf16[5,1,16,2,256,256]{5,4,3,2,1,0:T(8,128)(2,1)S(1)}, bf16[5,1,16,2,256,256]{5,4,3,2,1,0:T(8,128)(2,1)}, u32[]{:S(2)}) %copy-start.5) | copy-done | bytes 20971544
  278.4 5.0 %shard_map.88 = (bf16[4,256,256]{2,1,0:T(8,128)(2,1)S(1)}, bf16[4,256,256]{2,1,0:T(8,128)(2,1)S(1)}, bf16[4,256,256]{2,1,0:T(8,128)(2,1)S(1)}) custom-call(s32[16]{0:T(128)S(1)} %fusion.5.order, s32[5,16,2]{2,1,0:T(8,128)S(1)} %bitcast.163, bf16[11,256,256]{2,1,0:T(8,128)(2,1)S(1)} %bitcast_dynamic-update-slice_fusion.10.x_rows, ...), custom_call_target="tpu_custom_call" | custom-call | flops 805306368 | bytes 3145728 | tf_op jit(solution)/shard_map/pallas_call | solution.py:149
  287.1 2.5 shard_map.87.a
  289.6 4.3 %collective-permute-done.50.b = bf16[4,256,256]{2,1,0:T(8,128)(2,1)S(1)} collective-permute-done((bf16[4,256,256]{2,1,0:T(8,128)(2,1)S(1)}, bf16[4,256,256]{2,1,0:T(8,128)(2,1)S(1)}, u32[]{:S(2)}, u32[]{:S(2)}) %collective-permute-start.50) | collective-permute-done | bytes 524320 | tf_op jit(solution)/shard_map/ppermute | solution.py:31
  293.9 5.2 %collective-permute-done.51.c = bf16[4,256,256]{2,1,0:T(8,128)(2,1)S(1)} collective-permute-done((bf16[4,256,256]{2,1,0:T(8,128)(2,1)S(1)}, bf16[4,256,256]{2,1,0:T(8,128)(2,1)S(1)}, u32[]{:S(2)}, u32[]{:S(2)}) %collective-permute-start.51) | collective-permute-done | bytes 524320 | tf_op jit(solution)/shard_map/ppermute | solution.py:31
  300.6 3.2 collective-permute-start.54
  303.9 3.0 collective-permute-done.53.a
  307.7 2.5 collective-permute-done.55.c
  312.0 7.0 %copy-done.6 = bf16[5,1,16,2,256,256]{5,4,3,2,1,0:T(8,128)(2,1)S(1)} copy-done((bf16[5,1,16,2,256,256]{5,4,3,2,1,0:T(8,128)(2,1)S(1)}, bf16[5,1,16,2,256,256]{5,4,3,2,1,0:T(8,128)(2,1)}, u32[]{:S(2)}) %copy-start.6) | copy-done | bytes 20971544
  318.9 5.0 %shard_map.92 = (bf16[4,256,256]{2,1,0:T(8,128)(2,1)S(1)}, bf16[4,256,256]{2,1,0:T(8,128)(2,1)S(1)}, bf16[4,256,256]{2,1,0:T(8,128)(2,1)S(1)}) custom-call(s32[16]{0:T(128)S(1)} %fusion.5.order, s32[5,16,2]{2,1,0:T(8,128)S(1)} %bitcast.165, bf16[11,256,256]{2,1,0:T(8,128)(2,1)S(1)} %bitcast_dynamic-update-slice_fusion.8.x_rows, ...), custom_call_target="tpu_custom_call" | custom-call | flops 805306368 | bytes 3145728 | tf_op jit(solution)/shard_map/pallas_call | solution.py:149
  328.6 2.5 shard_map.91.a
  331.2 3.3 collective-permute-done.57.b
  334.4 5.2 %collective-permute-done.58.c = bf16[4,256,256]{2,1,0:T(8,128)(2,1)S(1)} collective-permute-done((bf16[4,256,256]{2,1,0:T(8,128)(2,1)S(1)}, bf16[4,256,256]{2,1,0:T(8,128)(2,1)S(1)}, u32[]{:S(2)}, u32[]{:S(2)}) %collective-permute-start.58) | collective-permute-done | bytes 524320 | tf_op jit(solution)/shard_map/ppermute | solution.py:31
  342.4 3.2 collective-permute-start.61
  345.8 3.0 collective-permute-done.60.a
  354.1 7.0 %copy-done.7 = bf16[5,1,16,2,256,256]{5,4,3,2,1,0:T(8,128)(2,1)S(1)} copy-done((bf16[5,1,16,2,256,256]{5,4,3,2,1,0:T(8,128)(2,1)S(1)}, bf16[5,1,16,2,256,256]{5,4,3,2,1,0:T(8,128)(2,1)}, u32[]{:S(2)}) %copy-start.7) | copy-done | bytes 20971544
  361.0 5.0 %shard_map.96 = (bf16[4,256,256]{2,1,0:T(8,128)(2,1)S(1)}, bf16[4,256,256]{2,1,0:T(8,128)(2,1)S(1)}, bf16[4,256,256]{2,1,0:T(8,128)(2,1)S(1)}) custom-call(s32[16]{0:T(128)S(1)} %fusion.5.order, s32[5,16,2]{2,1,0:T(8,128)S(1)} %bitcast.167, bf16[11,256,256]{2,1,0:T(8,128)(2,1)S(1)} %bitcast_dynamic-update-slice_fusion.6.x_rows, ...), custom_call_target="tpu_custom_call" | custom-call | flops 805306368 | bytes 3145728 | tf_op jit(solution)/shard_map/pallas_call | solution.py:149
  372.2 4.3 %collective-permute-done.64.b = bf16[4,256,256]{2,1,0:T(8,128)(2,1)S(1)} collective-permute-done((bf16[4,256,256]{2,1,0:T(8,128)(2,1)S(1)}, bf16[4,256,256]{2,1,0:T(8,128)(2,1)S(1)}, u32[]{:S(2)}, u32[]{:S(2)}) %collective-permute-start.64) | collective-permute-done | bytes 524320 | tf_op jit(solution)/shard_map/ppermute | solution.py:31
  376.5 5.2 %collective-permute-done.65.c = bf16[4,256,256]{2,1,0:T(8,128)(2,1)S(1)} collective-permute-done((bf16[4,256,256]{2,1,0:T(8,128)(2,1)S(1)}, bf16[4,256,256]{2,1,0:T(8,128)(2,1)S(1)}, u32[]{:S(2)}, u32[]{:S(2)}) %collective-permute-start.65) | collective-permute-done | bytes 524320 | tf_op jit(solution)/shard_map/ppermute | solution.py:31
  382.6 3.2 collective-permute-start.68
  385.8 2.9 collective-permute-done.67.a
  389.8 2.5 collective-permute-done.69.c
  (250 shorter events, 125.4 us)
Async XLA Ops:
  1.3 7.8 %collective-permute-start = (bf16[256,256]{0,1:T(8,128)(2,1)S(1)}, bf16[256,256]{0,1:T(8,128)(2,1)S(1)}, u32[]{:S(2)}, u32[]{:S(2)}) collective-permute-start(bf16[256,256]{0,1:T(8,128)(2,1)S(1)} %convolution_convert_fusion.1), channel_id=1, source_target_pairs={{0,8},{4,36},{8,16},{12,44},{16,24},{20,52},{24,0},{28,60},{32,40}... | collective-permute-start | bytes 393224 | tf_op jit(solution)/shard_map/ppermute | solution.py:31
  2.9 6.2 %collective-permute-start.1 = (bf16[256,256]{0,1:T(8,128)(2,1)S(1)}, bf16[256,256]{0,1:T(8,128)(2,1)S(1)}, u32[]{:S(2)}, u32[]{:S(2)}) collective-permute-start(bf16[256,256]{0,1:T(8,128)(2,1)S(1)} %convolution_convert_fusion.1), channel_id=1, source_target_pairs={{0,24},{4,100},{8,0},{12,108},{16,8},{20,116},{24,16},{28,124},{32... | collective-permute-start | bytes 393224 | tf_op jit(solution)/shard_map/ppermute | solution.py:31
  4.6 6.5 %collective-permute-start.2 = (bf16[256,256]{0,1:T(8,128)(2,1)S(1)}, bf16[256,256]{0,1:T(8,128)(2,1)S(1)}, u32[]{:S(2)}, u32[]{:S(2)}) collective-permute-start(bf16[256,256]{0,1:T(8,128)(2,1)S(1)} %convolution_convert_fusion.1), channel_id=1, source_target_pairs={{0,16},{4,68},{8,24},{12,76},{16,0},{20,84},{24,8},{28,92},{32,48}... | collective-permute-start | bytes 393224 | tf_op jit(solution)/shard_map/ppermute | solution.py:31
  11.9 18.1 %collective-permute-start.3 = (bf16[4,256,256]{1,2,0:T(8,128)(2,1)}, bf16[4,256,256]{1,2,0:T(8,128)(2,1)}, u32[]{:S(2)}, u32[]{:S(2)}) collective-permute-start(bf16[4,256,256]{1,2,0:T(8,128)(2,1)} %pad_maximum_fusion), channel_id=1, source_target_pairs={{0,32},{4,12},{8,40},{12,20},{16,48},{20,28},{24,56},{28,4},{32,64... | collective-permute-start | bytes 1572872 | tf_op jit(solution)/shard_map/ppermute | solution.py:31
  13.6 17.7 %collective-permute-start.4 = (bf16[4,256,256]{1,2,0:T(8,128)(2,1)}, bf16[4,256,256]{1,2,0:T(8,128)(2,1)}, u32[]{:S(2)}, u32[]{:S(2)}) collective-permute-start(bf16[4,256,256]{1,2,0:T(8,128)(2,1)} %pad_maximum_fusion), channel_id=1, source_target_pairs={{0,96},{4,28},{8,104},{12,4},{16,112},{20,12},{24,120},{28,20},{32... | collective-permute-start | bytes 1572872 | tf_op jit(solution)/shard_map/ppermute | solution.py:31
  15.2 18.2 %collective-permute-start.5 = (bf16[4,256,256]{1,2,0:T(8,128)(2,1)}, bf16[4,256,256]{1,2,0:T(8,128)(2,1)}, u32[]{:S(2)}, u32[]{:S(2)}) collective-permute-start(bf16[4,256,256]{1,2,0:T(8,128)(2,1)} %pad_maximum_fusion), channel_id=1, source_target_pairs={{0,64},{4,20},{8,72},{12,28},{16,80},{20,4},{24,88},{28,12},{32,96... | collective-permute-start | bytes 1572872 | tf_op jit(solution)/shard_map/ppermute | solution.py:31
  52.1 6.2 %collective-permute-start.7 = (bf16[256,256]{1,0:T(8,128)(2,1)S(1)}, bf16[256,256]{1,0:T(8,128)(2,1)S(1)}, u32[]{:S(2)}, u32[]{:S(2)}) collective-permute-start(bf16[256,256]{1,0:T(8,128)(2,1)S(1)} %shard_map.66), channel_id=1, source_target_pairs={{0,8},{4,36},{8,16},{12,44},{16,24},{20,52},{24,0},{28,60},{32,40}... | collective-permute-start | bytes 393224 | tf_op jit(solution)/shard_map/ppermute | solution.py:31
  52.5 6.9 %collective-permute-start.8 = (bf16[256,256]{1,0:T(8,128)(2,1)S(1)}, bf16[256,256]{1,0:T(8,128)(2,1)S(1)}, u32[]{:S(2)}, u32[]{:S(2)}) collective-permute-start(bf16[256,256]{1,0:T(8,128)(2,1)S(1)} %shard_map.66), channel_id=1, source_target_pairs={{0,24},{4,100},{8,0},{12,108},{16,8},{20,116},{24,16},{28,124},{32... | collective-permute-start | bytes 393224 | tf_op jit(solution)/shard_map/ppermute | solution.py:31
  55.5 6.5 %collective-permute-start.9 = (bf16[256,256]{1,0:T(8,128)(2,1)S(1)}, bf16[256,256]{1,0:T(8,128)(2,1)S(1)}, u32[]{:S(2)}, u32[]{:S(2)}) collective-permute-start(bf16[256,256]{1,0:T(8,128)(2,1)S(1)} %shard_map.66), channel_id=1, source_target_pairs={{0,16},{4,68},{8,24},{12,76},{16,0},{20,84},{24,8},{28,92},{32,48}... | collective-permute-start | bytes 393224 | tf_op jit(solution)/shard_map/ppermute | solution.py:31
  62.0 16.1 %collective-permute-start.10 = (bf16[4,256,256]{2,1,0:T(8,128)(2,1)S(1)}, bf16[4,256,256]{2,1,0:T(8,128)(2,1)S(1)}, u32[]{:S(2)}, u32[]{:S(2)}) collective-permute-start(bf16[4,256,256]{2,1,0:T(8,128)(2,1)S(1)} %pad_maximum_fusion.1.refs_2_), channel_id=1, source_target_pairs={{0,32},{4,12},{8,40},{12,20},{16,48},{20,28},{24,56},{28,4},{32,64... | collective-permute-start | bytes 1572872 | tf_op jit(solution)/shard_map/ppermute | solution.py:31
  62.7 15.3 %collective-permute-start.11 = (bf16[4,256,256]{2,1,0:T(8,128)(2,1)S(1)}, bf16[4,256,256]{2,1,0:T(8,128)(2,1)S(1)}, u32[]{:S(2)}, u32[]{:S(2)}) collective-permute-start(bf16[4,256,256]{2,1,0:T(8,128)(2,1)S(1)} %pad_maximum_fusion.1.refs_2_), channel_id=1, source_target_pairs={{0,96},{4,28},{8,104},{12,4},{16,112},{20,12},{24,120},{28,20},{32... | collective-permute-start | bytes 1572872 | tf_op jit(solution)/shard_map/ppermute | solution.py:31
  65.3 12.8 %collective-permute-start.12 = (bf16[4,256,256]{2,1,0:T(8,128)(2,1)S(1)}, bf16[4,256,256]{2,1,0:T(8,128)(2,1)S(1)}, u32[]{:S(2)}, u32[]{:S(2)}) collective-permute-start(bf16[4,256,256]{2,1,0:T(8,128)(2,1)S(1)} %pad_maximum_fusion.1.refs_2_), channel_id=1, source_target_pairs={{0,64},{4,20},{8,72},{12,28},{16,80},{20,4},{24,88},{28,12},{32,96... | collective-permute-start | bytes 1572872 | tf_op jit(solution)/shard_map/ppermute | solution.py:31
  84.9 6.2 %collective-permute-start.14 = (bf16[256,256]{1,0:T(8,128)(2,1)S(1)}, bf16[256,256]{1,0:T(8,128)(2,1)S(1)}, u32[]{:S(2)}, u32[]{:S(2)}) collective-permute-start(bf16[256,256]{1,0:T(8,128)(2,1)S(1)} %shard_map.69), channel_id=1, source_target_pairs={{0,8},{4,36},{8,16},{12,44},{16,24},{20,52},{24,0},{28,60},{32,40}... | collective-permute-start | bytes 393224 | tf_op jit(solution)/shard_map/ppermute | solution.py:31
  85.0 7.1 %collective-permute-start.15 = (bf16[256,256]{1,0:T(8,128)(2,1)S(1)}, bf16[256,256]{1,0:T(8,128)(2,1)S(1)}, u32[]{:S(2)}, u32[]{:S(2)}) collective-permute-start(bf16[256,256]{1,0:T(8,128)(2,1)S(1)} %shard_map.69), channel_id=1, source_target_pairs={{0,24},{4,100},{8,0},{12,108},{16,8},{20,116},{24,16},{28,124},{32... | collective-permute-start | bytes 393224 | tf_op jit(solution)/shard_map/ppermute | solution.py:31
  88.2 6.5 %collective-permute-start.16 = (bf16[256,256]{1,0:T(8,128)(2,1)S(1)}, bf16[256,256]{1,0:T(8,128)(2,1)S(1)}, u32[]{:S(2)}, u32[]{:S(2)}) collective-permute-start(bf16[256,256]{1,0:T(8,128)(2,1)S(1)} %shard_map.69), channel_id=1, source_target_pairs={{0,16},{4,68},{8,24},{12,76},{16,0},{20,84},{24,8},{28,92},{32,48}... | collective-permute-start | bytes 393224 | tf_op jit(solution)/shard_map/ppermute | solution.py:31
  94.8 10.5 %collective-permute-start.17 = (bf16[4,256,256]{2,1,0:T(8,128)(2,1)S(1)}, bf16[4,256,256]{2,1,0:T(8,128)(2,1)S(1)}, u32[]{:S(2)}, u32[]{:S(2)}) collective-permute-start(bf16[4,256,256]{2,1,0:T(8,128)(2,1)S(1)} %pad_maximum_fusion.2.refs_2_), channel_id=1, source_target_pairs={{0,32},{4,12},{8,40},{12,20},{16,48},{20,28},{24,56},{28,4},{32,64... | collective-permute-start | bytes 1572872 | tf_op jit(solution)/shard_map/ppermute | solution.py:31
  95.7 14.8 %collective-permute-start.18 = (bf16[4,256,256]{2,1,0:T(8,128)(2,1)S(1)}, bf16[4,256,256]{2,1,0:T(8,128)(2,1)S(1)}, u32[]{:S(2)}, u32[]{:S(2)}) collective-permute-start(bf16[4,256,256]{2,1,0:T(8,128)(2,1)S(1)} %pad_maximum_fusion.2.refs_2_), channel_id=1, source_target_pairs={{0,96},{4,28},{8,104},{12,4},{16,112},{20,12},{24,120},{28,20},{32... | collective-permute-start | bytes 1572872 | tf_op jit(solution)/shard_map/ppermute | solution.py:31
  98.2 14.2 %collective-permute-start.19 = (bf16[4,256,256]{2,1,0:T(8,128)(2,1)S(1)}, bf16[4,256,256]{2,1,0:T(8,128)(2,1)S(1)}, u32[]{:S(2)}, u32[]{:S(2)}) collective-permute-start(bf16[4,256,256]{2,1,0:T(8,128)(2,1)S(1)} %pad_maximum_fusion.2.refs_2_), channel_id=1, source_target_pairs={{0,64},{4,20},{8,72},{12,28},{16,80},{20,4},{24,88},{28,12},{32,96... | collective-permute-start | bytes 1572872 | tf_op jit(solution)/shard_map/ppermute | solution.py:31
  117.3 1.6 collective-permute-start.20
  119.1 6.2 %collective-permute-start.21 = (bf16[256,256]{1,0:T(8,128)(2,1)S(1)}, bf16[256,256]{1,0:T(8,128)(2,1)S(1)}, u32[]{:S(2)}, u32[]{:S(2)}) collective-permute-start(bf16[256,256]{1,0:T(8,128)(2,1)S(1)} %shard_map.72), channel_id=1, source_target_pairs={{0,8},{4,36},{8,16},{12,44},{16,24},{20,52},{24,0},{28,60},{32,40}... | collective-permute-start | bytes 393224 | tf_op jit(solution)/shard_map/ppermute | solution.py:31
  119.2 7.1 %collective-permute-start.22 = (bf16[256,256]{1,0:T(8,128)(2,1)S(1)}, bf16[256,256]{1,0:T(8,128)(2,1)S(1)}, u32[]{:S(2)}, u32[]{:S(2)}) collective-permute-start(bf16[256,256]{1,0:T(8,128)(2,1)S(1)} %shard_map.72), channel_id=1, source_target_pairs={{0,24},{4,100},{8,0},{12,108},{16,8},{20,116},{24,16},{28,124},{32... | collective-permute-start | bytes 393224 | tf_op jit(solution)/shard_map/ppermute | solution.py:31
  122.4 6.5 %collective-permute-start.23 = (bf16[256,256]{1,0:T(8,128)(2,1)S(1)}, bf16[256,256]{1,0:T(8,128)(2,1)S(1)}, u32[]{:S(2)}, u32[]{:S(2)}) collective-permute-start(bf16[256,256]{1,0:T(8,128)(2,1)S(1)} %shard_map.72), channel_id=1, source_target_pairs={{0,16},{4,68},{8,24},{12,76},{16,0},{20,84},{24,8},{28,92},{32,48}... | collective-permute-start | bytes 393224 | tf_op jit(solution)/shard_map/ppermute | solution.py:31
  129.0 10.5 %collective-permute-start.24 = (bf16[4,256,256]{2,1,0:T(8,128)(2,1)S(1)}, bf16[4,256,256]{2,1,0:T(8,128)(2,1)S(1)}, u32[]{:S(2)}, u32[]{:S(2)}) collective-permute-start(bf16[4,256,256]{2,1,0:T(8,128)(2,1)S(1)} %pad_maximum_fusion.3.refs_2_), channel_id=1, source_target_pairs={{0,32},{4,12},{8,40},{12,20},{16,48},{20,28},{24,56},{28,4},{32,64... | collective-permute-start | bytes 1572872 | tf_op jit(solution)/shard_map/ppermute | solution.py:31
  130.5 14.2 %collective-permute-start.25 = (bf16[4,256,256]{2,1,0:T(8,128)(2,1)S(1)}, bf16[4,256,256]{2,1,0:T(8,128)(2,1)S(1)}, u32[]{:S(2)}, u32[]{:S(2)}) collective-permute-start(bf16[4,256,256]{2,1,0:T(8,128)(2,1)S(1)} %pad_maximum_fusion.3.refs_2_), channel_id=1, source_target_pairs={{0,96},{4,28},{8,104},{12,4},{16,112},{20,12},{24,120},{28,20},{32... | collective-permute-start | bytes 1572872 | tf_op jit(solution)/shard_map/ppermute | solution.py:31
  132.3 12.9 %collective-permute-start.26 = (bf16[4,256,256]{2,1,0:T(8,128)(2,1)S(1)}, bf16[4,256,256]{2,1,0:T(8,128)(2,1)S(1)}, u32[]{:S(2)}, u32[]{:S(2)}) collective-permute-start(bf16[4,256,256]{2,1,0:T(8,128)(2,1)S(1)} %pad_maximum_fusion.3.refs_2_), channel_id=1, source_target_pairs={{0,64},{4,20},{8,72},{12,28},{16,80},{20,4},{24,88},{28,12},{32,96... | collective-permute-start | bytes 1572872 | tf_op jit(solution)/shard_map/ppermute | solution.py:31
  152.0 6.2 %collective-permute-start.28 = (bf16[256,256]{1,0:T(8,128)(2,1)S(1)}, bf16[256,256]{1,0:T(8,128)(2,1)S(1)}, u32[]{:S(2)}, u32[]{:S(2)}) collective-permute-start(bf16[256,256]{1,0:T(8,128)(2,1)S(1)} %shard_map.75), channel_id=1, source_target_pairs={{0,8},{4,36},{8,16},{12,44},{16,24},{20,52},{24,0},{28,60},{32,40}... | collective-permute-start | bytes 393224 | tf_op jit(solution)/shard_map/ppermute | solution.py:31
  152.1 7.1 %collective-permute-start.29 = (bf16[256,256]{1,0:T(8,128)(2,1)S(1)}, bf16[256,256]{1,0:T(8,128)(2,1)S(1)}, u32[]{:S(2)}, u32[]{:S(2)}) collective-permute-start(bf16[256,256]{1,0:T(8,128)(2,1)S(1)} %shard_map.75), channel_id=1, source_target_pairs={{0,24},{4,100},{8,0},{12,108},{16,8},{20,116},{24,16},{28,124},{32... | collective-permute-start | bytes 393224 | tf_op jit(solution)/shard_map/ppermute | solution.py:31
  155.3 6.5 %collective-permute-start.30 = (bf16[256,256]{1,0:T(8,128)(2,1)S(1)}, bf16[256,256]{1,0:T(8,128)(2,1)S(1)}, u32[]{:S(2)}, u32[]{:S(2)}) collective-permute-start(bf16[256,256]{1,0:T(8,128)(2,1)S(1)} %shard_map.75), channel_id=1, source_target_pairs={{0,16},{4,68},{8,24},{12,76},{16,0},{20,84},{24,8},{28,92},{32,48}... | collective-permute-start | bytes 393224 | tf_op jit(solution)/shard_map/ppermute | solution.py:31
  161.8 14.6 %collective-permute-start.31 = (bf16[4,256,256]{2,1,0:T(8,128)(2,1)S(1)}, bf16[4,256,256]{2,1,0:T(8,128)(2,1)}, u32[]{:S(2)}, u32[]{:S(2)}) collective-permute-start(bf16[4,256,256]{2,1,0:T(8,128)(2,1)S(1)} %pad_maximum_fusion.4.refs_2_), channel_id=1, source_target_pairs={{0,32},{4,12},{8,40},{12,20},{16,48},{20,28},{24,56},{28,4},{32,64... | collective-permute-start | bytes 1572872 | tf_op jit(solution)/shard_map/ppermute | solution.py:31
  163.3 14.2 %collective-permute-start.32 = (bf16[4,256,256]{2,1,0:T(8,128)(2,1)S(1)}, bf16[4,256,256]{2,1,0:T(8,128)(2,1)}, u32[]{:S(2)}, u32[]{:S(2)}) collective-permute-start(bf16[4,256,256]{2,1,0:T(8,128)(2,1)S(1)} %pad_maximum_fusion.4.refs_2_), channel_id=1, source_target_pairs={{0,96},{4,28},{8,104},{12,4},{16,112},{20,12},{24,120},{28,20},{32... | collective-permute-start | bytes 1572872 | tf_op jit(solution)/shard_map/ppermute | solution.py:31
  165.2 14.2 %collective-permute-start.33 = (bf16[4,256,256]{2,1,0:T(8,128)(2,1)S(1)}, bf16[4,256,256]{2,1,0:T(8,128)(2,1)}, u32[]{:S(2)}, u32[]{:S(2)}) collective-permute-start(bf16[4,256,256]{2,1,0:T(8,128)(2,1)S(1)} %pad_maximum_fusion.4.refs_2_), channel_id=1, source_target_pairs={{0,64},{4,20},{8,72},{12,28},{16,80},{20,4},{24,88},{28,12},{32,96... | collective-permute-start | bytes 1572872 | tf_op jit(solution)/shard_map/ppermute | solution.py:31
  185.3 1.8 collective-permute-start.34
  202.1 10.5 %collective-permute-start.36 = (bf16[4,256,256]{2,1,0:T(8,128)(2,1)S(1)}, bf16[4,256,256]{2,1,0:T(8,128)(2,1)S(1)}, u32[]{:S(2)}, u32[]{:S(2)}) collective-permute-start(bf16[4,256,256]{2,1,0:T(8,128)(2,1)S(1)} %get-tuple-element.168), channel_id=1, source_target_pairs={{0,32},{4,12},{8,40},{12,20},{16,48},{20,28},{24,56},{28,4},{32,64... | collective-permute-start | bytes 1572872 | tf_op jit(solution)/shard_map/ppermute | solution.py:31
  203.6 14.2 %collective-permute-start.37 = (bf16[4,256,256]{2,1,0:T(8,128)(2,1)S(1)}, bf16[4,256,256]{2,1,0:T(8,128)(2,1)S(1)}, u32[]{:S(2)}, u32[]{:S(2)}) collective-permute-start(bf16[4,256,256]{2,1,0:T(8,128)(2,1)S(1)} %get-tuple-element.169), channel_id=1, source_target_pairs={{0,96},{4,28},{8,104},{12,4},{16,112},{20,12},{24,120},{28,20},{32... | collective-permute-start | bytes 1572872 | tf_op jit(solution)/shard_map/ppermute | solution.py:31
  205.4 12.9 %collective-permute-start.38 = (bf16[4,256,256]{2,1,0:T(8,128)(2,1)S(1)}, bf16[4,256,256]{2,1,0:T(8,128)(2,1)S(1)}, u32[]{:S(2)}, u32[]{:S(2)}) collective-permute-start(bf16[4,256,256]{2,1,0:T(8,128)(2,1)S(1)} %get-tuple-element.170), channel_id=1, source_target_pairs={{0,64},{4,20},{8,72},{12,28},{16,80},{20,4},{24,88},{28,12},{32,96... | collective-permute-start | bytes 1572872 | tf_op jit(solution)/shard_map/ppermute | solution.py:31
  218.6 6.2 %collective-permute-start.39 = (bf16[256,256]{1,0:T(8,128)(2,1)S(1)}, bf16[256,256]{1,0:T(8,128)(2,1)S(1)}, u32[]{:S(2)}, u32[]{:S(2)}) collective-permute-start(bf16[256,256]{1,0:T(8,128)(2,1)S(1)} %get-tuple-element.208), channel_id=1, source_target_pairs={{0,8},{4,36},{8,16},{12,44},{16,24},{20,52},{24,0},{28,60},{32,40}... | collective-permute-start | bytes 393224 | tf_op jit(solution)/shard_map/ppermute | solution.py:31
  218.7 7.1 %collective-permute-start.40 = (bf16[256,256]{1,0:T(8,128)(2,1)S(1)}, bf16[256,256]{1,0:T(8,128)(2,1)S(1)}, u32[]{:S(2)}, u32[]{:S(2)}) collective-permute-start(bf16[256,256]{1,0:T(8,128)(2,1)S(1)} %get-tuple-element.207), channel_id=1, source_target_pairs={{0,24},{4,100},{8,0},{12,108},{16,8},{20,116},{24,16},{28,124},{32... | collective-permute-start | bytes 393224 | tf_op jit(solution)/shard_map/ppermute | solution.py:31
  221.9 6.5 %collective-permute-start.41 = (bf16[256,256]{1,0:T(8,128)(2,1)S(1)}, bf16[256,256]{1,0:T(8,128)(2,1)S(1)}, u32[]{:S(2)}, u32[]{:S(2)}) collective-permute-start(bf16[256,256]{1,0:T(8,128)(2,1)S(1)} %get-tuple-element.206), channel_id=1, source_target_pairs={{0,16},{4,68},{8,24},{12,76},{16,0},{20,84},{24,8},{28,92},{32,48}... | collective-permute-start | bytes 393224 | tf_op jit(solution)/shard_map/ppermute | solution.py:31
  242.1 10.5 %collective-permute-start.43 = (bf16[4,256,256]{2,1,0:T(8,128)(2,1)S(1)}, bf16[4,256,256]{2,1,0:T(8,128)(2,1)S(1)}, u32[]{:S(2)}, u32[]{:S(2)}) collective-permute-start(bf16[4,256,256]{2,1,0:T(8,128)(2,1)S(1)} %get-tuple-element.171), channel_id=1, source_target_pairs={{0,32},{4,12},{8,40},{12,20},{16,48},{20,28},{24,56},{28,4},{32,64... | collective-permute-start | bytes 1572872 | tf_op jit(solution)/shard_map/ppermute | solution.py:31
  243.5 14.2 %collective-permute-start.44 = (bf16[4,256,256]{2,1,0:T(8,128)(2,1)S(1)}, bf16[4,256,256]{2,1,0:T(8,128)(2,1)S(1)}, u32[]{:S(2)}, u32[]{:S(2)}) collective-permute-start(bf16[4,256,256]{2,1,0:T(8,128)(2,1)S(1)} %get-tuple-element.172), channel_id=1, source_target_pairs={{0,96},{4,28},{8,104},{12,4},{16,112},{20,12},{24,120},{28,20},{32... | collective-permute-start | bytes 1572872 | tf_op jit(solution)/shard_map/ppermute | solution.py:31
  245.4 14.1 %collective-permute-start.45 = (bf16[4,256,256]{2,1,0:T(8,128)(2,1)S(1)}, bf16[4,256,256]{2,1,0:T(8,128)(2,1)S(1)}, u32[]{:S(2)}, u32[]{:S(2)}) collective-permute-start(bf16[4,256,256]{2,1,0:T(8,128)(2,1)S(1)} %get-tuple-element.173), channel_id=1, source_target_pairs={{0,64},{4,20},{8,72},{12,28},{16,80},{20,4},{24,88},{28,12},{32,96... | collective-permute-start | bytes 1572872 | tf_op jit(solution)/shard_map/ppermute | solution.py:31
  259.8 6.2 %collective-permute-start.46 = (bf16[256,256]{1,0:T(8,128)(2,1)S(1)}, bf16[256,256]{1,0:T(8,128)(2,1)S(1)}, u32[]{:S(2)}, u32[]{:S(2)}) collective-permute-start(bf16[256,256]{1,0:T(8,128)(2,1)S(1)} %get-tuple-element.205), channel_id=1, source_target_pairs={{0,8},{4,36},{8,16},{12,44},{16,24},{20,52},{24,0},{28,60},{32,40}... | collective-permute-start | bytes 393224 | tf_op jit(solution)/shard_map/ppermute | solution.py:31
  259.9 7.1 %collective-permute-start.47 = (bf16[256,256]{1,0:T(8,128)(2,1)S(1)}, bf16[256,256]{1,0:T(8,128)(2,1)S(1)}, u32[]{:S(2)}, u32[]{:S(2)}) collective-permute-start(bf16[256,256]{1,0:T(8,128)(2,1)S(1)} %get-tuple-element.204), channel_id=1, source_target_pairs={{0,24},{4,100},{8,0},{12,108},{16,8},{20,116},{24,16},{28,124},{32... | collective-permute-start | bytes 393224 | tf_op jit(solution)/shard_map/ppermute | solution.py:31
  263.1 6.5 %collective-permute-start.48 = (bf16[256,256]{1,0:T(8,128)(2,1)S(1)}, bf16[256,256]{1,0:T(8,128)(2,1)S(1)}, u32[]{:S(2)}, u32[]{:S(2)}) collective-permute-start(bf16[256,256]{1,0:T(8,128)(2,1)S(1)} %get-tuple-element.203), channel_id=1, source_target_pairs={{0,16},{4,68},{8,24},{12,76},{16,0},{20,84},{24,8},{28,92},{32,48}... | collective-permute-start | bytes 393224 | tf_op jit(solution)/shard_map/ppermute | solution.py:31
  269.8 1.6 collective-permute-start.49
  283.5 10.5 %collective-permute-start.50 = (bf16[4,256,256]{2,1,0:T(8,128)(2,1)S(1)}, bf16[4,256,256]{2,1,0:T(8,128)(2,1)S(1)}, u32[]{:S(2)}, u32[]{:S(2)}) collective-permute-start(bf16[4,256,256]{2,1,0:T(8,128)(2,1)S(1)} %get-tuple-element.174), channel_id=1, source_target_pairs={{0,32},{4,12},{8,40},{12,20},{16,48},{20,28},{24,56},{28,4},{32,64... | collective-permute-start | bytes 1572872 | tf_op jit(solution)/shard_map/ppermute | solution.py:31
  285.0 14.2 %collective-permute-start.51 = (bf16[4,256,256]{2,1,0:T(8,128)(2,1)S(1)}, bf16[4,256,256]{2,1,0:T(8,128)(2,1)S(1)}, u32[]{:S(2)}, u32[]{:S(2)}) collective-permute-start(bf16[4,256,256]{2,1,0:T(8,128)(2,1)S(1)} %get-tuple-element.175), channel_id=1, source_target_pairs={{0,96},{4,28},{8,104},{12,4},{16,112},{20,12},{24,120},{28,20},{32... | collective-permute-start | bytes 1572872 | tf_op jit(solution)/shard_map/ppermute | solution.py:31
  286.8 12.9 %collective-permute-start.52 = (bf16[4,256,256]{2,1,0:T(8,128)(2,1)S(1)}, bf16[4,256,256]{2,1,0:T(8,128)(2,1)S(1)}, u32[]{:S(2)}, u32[]{:S(2)}) collective-permute-start(bf16[4,256,256]{2,1,0:T(8,128)(2,1)S(1)} %get-tuple-element.176), channel_id=1, source_target_pairs={{0,64},{4,20},{8,72},{12,28},{16,80},{20,4},{24,88},{28,12},{32,96... | collective-permute-start | bytes 1572872 | tf_op jit(solution)/shard_map/ppermute | solution.py:31
  300.6 6.4 %collective-permute-start.53 = (bf16[256,256]{1,0:T(8,128)(2,1)}, bf16[256,256]{1,0:T(8,128)(2,1)S(1)}, u32[]{:S(2)}, u32[]{:S(2)}) collective-permute-start(bf16[256,256]{1,0:T(8,128)(2,1)} %get-tuple-element.202), channel_id=1, source_target_pairs={{0,8},{4,36},{8,16},{12,44},{16,24},{20,52},{24,0},{28,60},{32,40}... | collective-permute-start | bytes 393224 | tf_op jit(solution)/shard_map/ppermute | solution.py:31
  300.6 7.2 %collective-permute-start.54 = (bf16[256,256]{1,0:T(8,128)(2,1)S(1)}, bf16[256,256]{1,0:T(8,128)(2,1)S(1)}, u32[]{:S(2)}, u32[]{:S(2)}) collective-permute-start(bf16[256,256]{1,0:T(8,128)(2,1)S(1)} %get-tuple-element.201), channel_id=1, source_target_pairs={{0,24},{4,100},{8,0},{12,108},{16,8},{20,116},{24,16},{28,124},{32... | collective-permute-start | bytes 393224 | tf_op jit(solution)/shard_map/ppermute | solution.py:31
  303.8 6.5 %collective-permute-start.55 = (bf16[256,256]{1,0:T(8,128)(2,1)S(1)}, bf16[256,256]{1,0:T(8,128)(2,1)S(1)}, u32[]{:S(2)}, u32[]{:S(2)}) collective-permute-start(bf16[256,256]{1,0:T(8,128)(2,1)S(1)} %get-tuple-element.200), channel_id=1, source_target_pairs={{0,16},{4,68},{8,24},{12,76},{16,0},{20,84},{24,8},{28,92},{32,48}... | collective-permute-start | bytes 393224 | tf_op jit(solution)/shard_map/ppermute | solution.py:31
  324.0 10.5 %collective-permute-start.57 = (bf16[4,256,256]{2,1,0:T(8,128)(2,1)S(1)}, bf16[4,256,256]{2,1,0:T(8,128)(2,1)S(1)}, u32[]{:S(2)}, u32[]{:S(2)}) collective-permute-start(bf16[4,256,256]{2,1,0:T(8,128)(2,1)S(1)} %get-tuple-element.177), channel_id=1, source_target_pairs={{0,32},{4,12},{8,40},{12,20},{16,48},{20,28},{24,56},{28,4},{32,64... | collective-permute-start | bytes 1572872 | tf_op jit(solution)/shard_map/ppermute | solution.py:31
  325.5 14.2 %collective-permute-start.58 = (bf16[4,256,256]{2,1,0:T(8,128)(2,1)S(1)}, bf16[4,256,256]{2,1,0:T(8,128)(2,1)S(1)}, u32[]{:S(2)}, u32[]{:S(2)}) collective-permute-start(bf16[4,256,256]{2,1,0:T(8,128)(2,1)S(1)} %get-tuple-element.178), channel_id=1, source_target_pairs={{0,96},{4,28},{8,104},{12,4},{16,112},{20,12},{24,120},{28,20},{32... | collective-permute-start | bytes 1572872 | tf_op jit(solution)/shard_map/ppermute | solution.py:31
  327.3 14.1 %collective-permute-start.59 = (bf16[4,256,256]{2,1,0:T(8,128)(2,1)S(1)}, bf16[4,256,256]{2,1,0:T(8,128)(2,1)S(1)}, u32[]{:S(2)}, u32[]{:S(2)}) collective-permute-start(bf16[4,256,256]{2,1,0:T(8,128)(2,1)S(1)} %get-tuple-element.179), channel_id=1, source_target_pairs={{0,64},{4,20},{8,72},{12,28},{16,80},{20,4},{24,88},{28,12},{32,96... | collective-permute-start | bytes 1572872 | tf_op jit(solution)/shard_map/ppermute | solution.py:31
  342.4 6.4 %collective-permute-start.60 = (bf16[256,256]{1,0:T(8,128)(2,1)}, bf16[256,256]{1,0:T(8,128)(2,1)S(1)}, u32[]{:S(2)}, u32[]{:S(2)}) collective-permute-start(bf16[256,256]{1,0:T(8,128)(2,1)} %get-tuple-element.199), channel_id=1, source_target_pairs={{0,8},{4,36},{8,16},{12,44},{16,24},{20,52},{24,0},{28,60},{32,40}... | collective-permute-start | bytes 393224 | tf_op jit(solution)/shard_map/ppermute | solution.py:31
  342.4 7.5 %collective-permute-start.61 = (bf16[256,256]{1,0:T(8,128)(2,1)}, bf16[256,256]{1,0:T(8,128)(2,1)S(1)}, u32[]{:S(2)}, u32[]{:S(2)}) collective-permute-start(bf16[256,256]{1,0:T(8,128)(2,1)} %get-tuple-element.198), channel_id=1, source_target_pairs={{0,24},{4,100},{8,0},{12,108},{16,8},{20,116},{24,16},{28,124},{32... | collective-permute-start | bytes 393224 | tf_op jit(solution)/shard_map/ppermute | solution.py:31
  345.7 6.5 %collective-permute-start.62 = (bf16[256,256]{1,0:T(8,128)(2,1)S(1)}, bf16[256,256]{1,0:T(8,128)(2,1)S(1)}, u32[]{:S(2)}, u32[]{:S(2)}) collective-permute-start(bf16[256,256]{1,0:T(8,128)(2,1)S(1)} %get-tuple-element.197), channel_id=1, source_target_pairs={{0,16},{4,68},{8,24},{12,76},{16,0},{20,84},{24,8},{28,92},{32,48}... | collective-permute-start | bytes 393224 | tf_op jit(solution)/shard_map/ppermute | solution.py:31
  352.3 1.7 collective-permute-start.63
  366.0 10.5 %collective-permute-start.64 = (bf16[4,256,256]{2,1,0:T(8,128)(2,1)S(1)}, bf16[4,256,256]{2,1,0:T(8,128)(2,1)S(1)}, u32[]{:S(2)}, u32[]{:S(2)}) collective-permute-start(bf16[4,256,256]{2,1,0:T(8,128)(2,1)S(1)} %get-tuple-element.180), channel_id=1, source_target_pairs={{0,32},{4,12},{8,40},{12,20},{16,48},{20,28},{24,56},{28,4},{32,64... | collective-permute-start | bytes 1572872 | tf_op jit(solution)/shard_map/ppermute | solution.py:31
  367.5 14.2 %collective-permute-start.65 = (bf16[4,256,256]{2,1,0:T(8,128)(2,1)S(1)}, bf16[4,256,256]{2,1,0:T(8,128)(2,1)S(1)}, u32[]{:S(2)}, u32[]{:S(2)}) collective-permute-start(bf16[4,256,256]{2,1,0:T(8,128)(2,1)S(1)} %get-tuple-element.181), channel_id=1, source_target_pairs={{0,96},{4,28},{8,104},{12,4},{16,112},{20,12},{24,120},{28,20},{32... | collective-permute-start | bytes 1572872 | tf_op jit(solution)/shard_map/ppermute | solution.py:31
  369.4 12.9 %collective-permute-start.66 = (bf16[4,256,256]{2,1,0:T(8,128)(2,1)S(1)}, bf16[4,256,256]{2,1,0:T(8,128)(2,1)S(1)}, u32[]{:S(2)}, u32[]{:S(2)}) collective-permute-start(bf16[4,256,256]{2,1,0:T(8,128)(2,1)S(1)} %get-tuple-element.182), channel_id=1, source_target_pairs={{0,64},{4,20},{8,72},{12,28},{16,80},{20,4},{24,88},{28,12},{32,96... | collective-permute-start | bytes 1572872 | tf_op jit(solution)/shard_map/ppermute | solution.py:31
  382.5 6.2 %collective-permute-start.67 = (bf16[256,256]{1,0:T(8,128)(2,1)S(1)}, bf16[256,256]{1,0:T(8,128)(2,1)S(1)}, u32[]{:S(2)}, u32[]{:S(2)}) collective-permute-start(bf16[256,256]{1,0:T(8,128)(2,1)S(1)} %get-tuple-element.196), channel_id=1, source_target_pairs={{0,8},{4,36},{8,16},{12,44},{16,24},{20,52},{24,0},{28,60},{32,40}... | collective-permute-start | bytes 393224 | tf_op jit(solution)/shard_map/ppermute | solution.py:31
  382.6 7.1 %collective-permute-start.68 = (bf16[256,256]{1,0:T(8,128)(2,1)S(1)}, bf16[256,256]{1,0:T(8,128)(2,1)S(1)}, u32[]{:S(2)}, u32[]{:S(2)}) collective-permute-start(bf16[256,256]{1,0:T(8,128)(2,1)S(1)} %get-tuple-element.195), channel_id=1, source_target_pairs={{0,24},{4,100},{8,0},{12,108},{16,8},{20,116},{24,16},{28,124},{32... | collective-permute-start | bytes 393224 | tf_op jit(solution)/shard_map/ppermute | solution.py:31
  385.8 6.5 %collective-permute-start.69 = (bf16[256,256]{1,0:T(8,128)(2,1)S(1)}, bf16[256,256]{1,0:T(8,128)(2,1)S(1)}, u32[]{:S(2)}, u32[]{:S(2)}) collective-permute-start(bf16[256,256]{1,0:T(8,128)(2,1)S(1)} %get-tuple-element.194), channel_id=1, source_target_pairs={{0,16},{4,68},{8,24},{12,76},{16,0},{20,84},{24,8},{28,92},{32,48}... | collective-permute-start | bytes 393224 | tf_op jit(solution)/shard_map/ppermute | solution.py:31
  (43 other events, 611.9 us)
